TPU v7x, 32 devices: a whole 2x2x4 slice. The times are simulated.
32 devices in a mesh: gx: 8 (over z, y), gy: 2 (over x), gz: 2 (over core).
Axes of the slice: x: 2, y: 2, z: 4, core: 2. Of those that a mesh axis runs over, the one named last changes fastest.
Arguments:
- pops: float32 [19, 32, 64, 256], P(None, 'gz', 'gx', 'gy'), as said below
- solid: int32 [32, 64, 256], P('gz', 'gx', 'gy'), may hold values 0 or 1
- surf_cell: int32 [2, 8, 2, 512], P('gz', 'gx', 'gy'), may hold values from 0 to 16383
- surf_panel: int32 [2, 8, 2, 512], P('gz', 'gx', 'gy'), may hold values from -1 to 39, as said below
- surf_area: float32 [2, 8, 2, 512], P('gz', 'gx', 'gy'), may hold values from 0.1 to 1
- mode_shape: float32 [2, 8, 2, 12, 512], P('gz', 'gx', 'gy'), may hold values from -5 to 5
- mode_of_panel: int32 [40], replicated, may hold values from 0 to 11
- compliance: float32 [12], replicated, may hold values from 0.3 to 3
Outputs:
- read: float32 [19, 32, 64, 256], P(None, 'gz', 'gx', 'gy')
- panel_force: float32 [40], replicated
- mode_amplitude: float32 [12], replicated
Inputs may be any that keep to these rules, and one draw needn't show every extreme that they name: pops is positive, with densities near 1 and flow speeds below 0.25. `surf_panel`: -1 marks an empty slot; on each device the live slots come first, at least 64 of them; some device has all 512 slots live; one panel's surfels lie on at most about 40 consecutive bricks in the linear order (vertical, streamwise, crosswise) of the devices, counted periodically so that the last brick is followed by the first.
All inputs are finite; a program needn't handle non-finite values. No bound on the sum of `solid` on one device may be relied on, other than what follows from the above.
Results may differ from a plain program's by a relative error of at most 0.00011.
Values sent between devices are 32-bit elements; how exact they have to be, the bound alone decides.
A program may use at most 64 MiB of HBM per device.

v0:
```python
import jax
import jax.numpy as jnp
from jax import lax
from jax.sharding import PartitionSpec as P

PANELS = 40
MODES = 12


VELOCITY = (
    (0, 0, 0),
    (1, 0, 0),
    (-1, 0, 0),
    (0, 1, 0),
    (0, -1, 0),
    (0, 0, 1),
    (0, 0, -1),
    (1, 1, 0),
    (-1, -1, 0),
    (1, -1, 0),
    (-1, 1, 0),
    (1, 0, 1),
    (-1, 0, -1),
    (1, 0, -1),
    (-1, 0, 1),
    (0, 1, 1),
    (0, -1, -1),
    (0, 1, -1),
    (0, -1, 1),
)
WEIGHTS = (1.0 / 3.0,) + (1.0 / 18.0,) * 6 + (1.0 / 36.0,) * 12
OPPOSITE = (0, 2, 1, 4, 3, 6, 5, 8, 7, 10, 9, 12, 11, 14, 13, 16, 15, 18, 17)
OMEGA = 1.0 / 0.6
WALL_SCALE = 0.02


def padded_2(block, sides, width):
    for axis, dim in sides:
        count = lax.axis_size(axis)
        forward = [(i, i + 1) for i in range(count - 1)]
        forward.append((count - 1, 0))
        backward = [(target, source) for source, target in forward]
        low = lax.ppermute(
            lax.slice_in_dim(block, block.shape[dim] - width, None, axis=dim), axis, forward
        )
        high = lax.ppermute(lax.slice_in_dim(block, 0, width, axis=dim), axis, backward)
        block = jnp.concatenate([low, block, high], axis=dim)
    return block


def collide(pops, solid):
    density = pops[0]
    for index in range(1, 19):
        density = density + pops[index]
    moments = []
    for axis in range(3):
        total = jnp.zeros_like(density)
        for index in range(19):
            comp = VELOCITY[index][axis]
            if comp == 1:
                total = total + pops[index]
            elif comp == -1:
                total = total - pops[index]
        moments.append(total / density)
    squared = moments[0] * moments[0] + moments[1] * moments[1] + moments[2] * moments[2]
    result = []
    for index in range(19):
        projected = jnp.zeros_like(density)
        for axis in range(3):
            comp = VELOCITY[index][axis]
            if comp == 1:
                projected = projected + moments[axis]
            elif comp == -1:
                projected = projected - moments[axis]
        equilib = (
            WEIGHTS[index]
            * density
            * (1.0 + 3.0 * projected + 4.5 * projected * projected - 1.5 * squared)
        )
        relaxed = pops[index] + OMEGA * (equilib - pops[index])
        result.append(jnp.where(solid == 1, pops[OPPOSITE[index]], relaxed))
    return (density, result)


def stream_joint(pieces):
    field = jnp.stack(pieces)
    depth, rows, width = (field.shape[1], field.shape[2], field.shape[3])
    padded = padded_2(field, (("gx", 2), ("gy", 3), ("gz", 1)), 1)
    result = []
    for index in range(19):
        vel = VELOCITY[index]
        result.append(
            padded[
                index,
                1 - vel[2] : 1 - vel[2] + depth,
                1 - vel[0] : 1 - vel[0] + rows,
                1 - vel[1] : 1 - vel[1] + width,
            ]
        )
    return result


def stream_all(pieces):
    return stream_joint(pieces)


def per_device(
    pops, solid, surf_cell, surf_panel, surf_area, mode_shape, mode_of_panel, compliance
):
    depth, rows, width = (pops.shape[1], pops.shape[2], pops.shape[3])
    density, post = collide(pops, solid)
    flat_density = density.reshape(-1)
    cell_list = surf_cell.reshape(-1)
    panel_list = surf_panel.reshape(-1)
    gathered = flat_density[cell_list]
    live = panel_list >= 0
    contrib = jnp.where(live, surf_area.reshape(-1) * ((gathered - 1.0) / 3.0), 0.0)
    panel_ids = jnp.arange(PANELS, dtype=jnp.int32)
    partial_force = jnp.sum(
        jnp.where(panel_list[:, None] == panel_ids[None, :], contrib[:, None], 0.0), axis=0
    )
    panel_force = lax.psum(partial_force, ("gx", "gy", "gz"))
    mode_ids = jnp.arange(MODES, dtype=jnp.int32)
    mode_load = jnp.sum(
        jnp.where(mode_of_panel[:, None] == mode_ids[None, :], panel_force[:, None], 0.0), axis=0
    )
    mode_amplitude = compliance * mode_load
    shapes = mode_shape.reshape(MODES, -1)
    wall = WALL_SCALE * jnp.sum(mode_amplitude[:, None] * shapes, axis=0)
    values = jnp.where(live, gathered * wall, 0.0)
    wall_flux = jnp.zeros_like(flat_density).at[cell_list].add(values).reshape(depth, rows, width)
    corrected = []
    for index in range(19):
        coef = 6.0 * WEIGHTS[index] * VELOCITY[index][0]
        corrected.append(post[index] + coef * wall_flux)
    result = stream_all(corrected)
    return (jnp.stack(result), panel_force, mode_amplitude)


def solution(mesh):
    placed = (
        P(None, "gz", "gx", "gy"),
        P("gz", "gx", "gy"),
        P("gz", "gx", "gy", None),
        P("gz", "gx", "gy", None),
        P("gz", "gx", "gy", None),
        P("gz", "gx", "gy", None, None),
        P(),
        P(),
    )
    return jax.shard_map(
        per_device,
        mesh=mesh,
        in_specs=placed,
        out_specs=(P(None, "gz", "gx", "gy"), P(), P()),
        check_vma=False,
    )
```

profile of v0, /device:TPU:0, one launch (start us, length us, event | category | flops | bytes accessed | tf_op | source)
XLA Modules:
  0.0 97.8 jit_solution(2532107182724770170)
XLA Ops:
  1.3 1.4 %bitcast_add_fusion = f32[16384]{0:T(1024)S(1)} fusion(f32[19,16,8,128]{3,2,1,0:T(8,128)} %param.8), kind=kLoop, calls=%fused_computation.249 | loop fusion | flops 294912 | bytes 1310720 | tf_op jit(solution)/shard_map/add | solution.py:54
  2.8 3.1 %gather_fusion = f32[512]{0:T(512)S(1)} fusion(f32[16384]{0:T(1024)S(1)} %bitcast_add_fusion, s32[1024]{0:T(1024)S(1)} %pad_clamp_fusion), kind=kCustom, calls=%fused_computation | custom fusion | bytes 6144 | tf_op jit(solution)/shard_map/gather | solution.py:115
  6.1 42.0 %psum.7 = f32[40]{0:T(128)S(1)} all-reduce(f32[40]{0:T(128)S(1)} %select_reduce_fusion), channel_id=1, replica_groups=mesh['gx'=8,'gy'=2,'gz'=2] {'gx','gy','gz'}, use_global_device_ids=true, to_apply=%region_1.2 | all-reduce | flops 40 | bytes 320 | tf_op jit(solution)/shard_map/psum | solution.py:122
  48.4 3.3 %scatter_custom_fusion = f32[16384]{0:T(1024)S(1)} fusion(s32[512]{0:T(512)S(1)} %bitcast.409, f32[512]{0:T(512)S(1)} %multiply_select_fusion, f32[]{:T(128)} %constant.4.clone.1), kind=kCustom, calls=%fused_computation.305 | custom fusion | flops 512 | bytes 65540 | tf_op jit(solution)/shard_map/scatter-add | solution.py:131
  53.1 2.3 %collective-permute-start = (f32[19,16,1,128]{3,1,2,0:T(8,128)S(1)}, f32[19,16,1,128]{3,1,2,0:T(8,128)S(1)}, u32[]{:S(2)}, u32[]{:S(2)}) collective-permute-start(f32[19,16,1,128]{3,1,2,0:T(8,128)S(1)} %bitcast.405), channel_id=1, source_target_pairs={{0,4},{4,8},{8,12},{12,16},{16,20},{20,24},{24,28},{28,0},{1,5},{5... | collective-permute-start | bytes 466952 | tf_op jit(solution)/shard_map/ppermute | solution.py:43
  55.4 2.5 %collective-permute-start.1 = (f32[19,16,1,128]{3,1,2,0:T(8,128)S(1)}, f32[19,16,1,128]{3,1,2,0:T(8,128)S(1)}, u32[]{:S(2)}, u32[]{:S(2)}) collective-permute-start(f32[19,16,1,128]{3,1,2,0:T(8,128)S(1)} %bitcast.404), channel_id=1, source_target_pairs={{4,0},{8,4},{12,8},{16,12},{20,16},{24,20},{28,24},{0,28},{5,1},{9... | collective-permute-start | bytes 466952 | tf_op jit(solution)/shard_map/ppermute | solution.py:46
  57.9 3.3 %collective-permute-done = f32[19,16,1,128]{3,1,2,0:T(8,128)S(1)} collective-permute-done((f32[19,16,1,128]{3,1,2,0:T(8,128)S(1)}, f32[19,16,1,128]{3,1,2,0:T(8,128)S(1)}, u32[]{:S(2)}, u32[]{:S(2)}) %collective-permute-start) | collective-permute-done | bytes 155680 | tf_op jit(solution)/shard_map/ppermute | solution.py:43
  61.2 1.3 %collective-permute-done.1 = f32[19,16,1,128]{3,1,2,0:T(8,128)S(1)} collective-permute-done((f32[19,16,1,128]{3,1,2,0:T(8,128)S(1)}, f32[19,16,1,128]{3,1,2,0:T(8,128)S(1)}, u32[]{:S(2)}, u32[]{:S(2)}) %collective-permute-start.1) | collective-permute-done | bytes 155680 | tf_op jit(solution)/shard_map/ppermute | solution.py:46
  63.0 3.1 %fusion.174 = (f32[19,16,10,1]{3,2,1,0:T(8,128)}, f32[19,16,10,1]{3,2,1,0:T(8,128)}) fusion(f32[19,16,10,128]{3,2,1,0:T(8,128)S(1)} %pad_maximum_fusion), kind=kLoop, calls=%fused_computation.315 | loop fusion | bytes 48640 | tf_op jit(solution)/shard_map/slice | solution.py:46
  66.1 2.8 %copy.56 = f32[19,16,10,1]{0,1,3,2:T(8,128)S(1)} copy(f32[19,16,10,1]{3,2,1,0:T(8,128)} %get-tuple-element.18) | data formatting | bytes 24320 | tf_op jit(solution)/shard_map/slice | solution.py:44
  68.9 2.1 %collective-permute-start.2 = (f32[19,16,10,1]{0,1,3,2:T(8,128)S(1)}, f32[19,16,10,1]{0,1,3,2:T(8,128)S(1)}, u32[]{:S(2)}, u32[]{:S(2)}) collective-permute-start(f32[19,16,10,1]{0,1,3,2:T(8,128)S(1)} %copy.56), channel_id=1, source_target_pairs={{0,2},{2,0},{1,3},{3,1},{4,6},{6,4},{5,7},{7,5},{8,10},{10,8},{9,1... | collective-permute-start | bytes 36488 | tf_op jit(solution)/shard_map/ppermute | solution.py:43
  71.6 2.8 %copy.58 = f32[19,16,10,1]{0,1,3,2:T(8,128)S(1)} copy(f32[19,16,10,1]{3,2,1,0:T(8,128)} %get-tuple-element.17) | data formatting | bytes 24320 | tf_op jit(solution)/shard_map/slice | solution.py:46
  74.5 3.7 %copy.57 = f32[19,16,10,1]{3,2,1,0:T(8,128)} copy(f32[19,16,10,1]{0,1,3,2:T(8,128)S(1)} %collective-permute-done.2) | data formatting | bytes 24320 | tf_op jit(solution)/shard_map/ppermute | solution.py:43
  78.2 1.6 %constant_dynamic-update-slice_fusion.34 = f32[19,16,8,128]{3,2,1,0:T(8,128)} fusion(f32[19,16,8,128]{3,2,1,0:T(8,128)} %constant_dynamic-update-slice_fusion.35, f32[19,16,10,1]{3,2,1,0:T(8,128)} %copy.57, f32[19,16,1,128]{3,2,1,0:T(1,128)S(1)} %bitcast.387, f32[19,16,8,128]{3,2,1,0:T(8,128)S(1)} %constant_dynamic-update-slice_fusion, ...), kind=kLoop, calls=%fused_computation.63 | loop fusion | flops 49152 | bytes 4112384
  79.9 3.7 %copy.59 = f32[19,16,10,1]{3,2,1,0:T(8,128)} copy(f32[19,16,10,1]{0,1,3,2:T(8,128)S(1)} %collective-permute-done.3) | data formatting | bytes 24320 | tf_op jit(solution)/shard_map/ppermute | solution.py:46
  83.6 1.8 %pad_maximum_fusion.1 = (f32[19,1,10,130]{3,2,1,0:T(8,128)S(1)}, f32[19,1,10,130]{3,2,1,0:T(8,128)S(1)}) fusion(f32[19,16,10,1]{3,2,1,0:T(8,128)} %copy.59, f32[19,16,10,1]{3,2,1,0:T(8,128)} %copy.57, f32[19,16,1,128]{3,2,1,0:T(1,128)S(1)} %bitcast.388, f32[19,16,8,128]{3,2,1,0:T(8,128)S(1)} %constant_dynamic-update-slice_fusion, ...), kind=kLoop, calls=%fused_computation.3 | loop fusion | flops 197600 | bytes 1778400 | tf_op jit(solution)/shard_map/concatenate | solution.py:47
  85.9 0.8 constant_dynamic-update-slice_fusion.33
  86.7 0.8 collective-permute-done.4
  88.9 0.7 constant_dynamic-update-slice_fusion.30
  89.7 0.8 constant_dynamic-update-slice_fusion.29
  90.4 0.8 constant_dynamic-update-slice_fusion.28
  91.2 0.8 constant_dynamic-update-slice_fusion.27
  95.5 0.8 constant_dynamic-update-slice_fusion.21
  97.0 0.8 constant_dynamic-update-slice_fusion.19
  (71 shorter events, 9.9 us)
Async XLA Ops:
  2.7 3.2 %copy-start.6 = (s32[1,1,1,512]{3,2,1,0:T(1,128)S(1)}, s32[1,1,1,512]{3,2,1,0:T(1,128)}, u32[]{:S(2)}) copy-start(s32[1,1,1,512]{3,2,1,0:T(1,128)} %param.11) | copy-start | bytes 6148
  2.7 3.2 %copy-start.7 = (f32[1,1,1,512]{3,2,1,0:T(1,128)S(1)}, f32[1,1,1,512]{3,2,1,0:T(1,128)}, u32[]{:S(2)}) copy-start(f32[1,1,1,512]{3,2,1,0:T(1,128)} %param.12) | copy-start | bytes 6148
  2.7 45.4 %copy-start.9 = (s32[40]{0:T(128)S(1)}, s32[40]{0:T(128)}, u32[]{:S(2)}) copy-start(s32[40]{0:T(128)} %param.14) | copy-start | bytes 484
  2.7 45.5 %copy-start.10 = (f32[12]{0:T(128)S(1)}, f32[12]{0:T(128)}, u32[]{:S(2)}) copy-start(f32[12]{0:T(128)} %param.15) | copy-start | bytes 148
  2.7 45.5 %copy-start.5 = (f32[1,1,1,12,512]{4,2,3,1,0:T(1,128)S(1)}, f32[1,1,1,12,512]{4,2,3,1,0:T(1,128)}, u32[]{:S(2)}) copy-start(f32[1,1,1,12,512]{4,2,3,1,0:T(1,128)} %param.13) | copy-start | bytes 73732
  2.8 48.9 %copy-start.2 = (f32[19,16,8,128]{3,2,1,0:T(8,128)S(1)}, f32[19,16,8,128]{3,2,1,0:T(8,128)}, u32[]{:S(2)}) copy-start(f32[19,16,8,128]{3,2,1,0:T(8,128)} %param.8) | copy-start | bytes 3735556
  2.8 48.9 %copy-start.4 = (s32[16,8,128]{2,1,0:T(8,128)S(1)}, s32[16,8,128]{2,1,0:T(8,128)}, u32[]{:S(2)}) copy-start(s32[16,8,128]{2,1,0:T(8,128)} %param.9) | copy-start | bytes 196612
  48.1 3.9 %copy-start.11 = (f32[40]{0:T(128)}, f32[40]{0:T(128)S(1)}, u32[]{:S(2)}) copy-start(f32[40]{0:T(128)S(1)} %psum.7) | copy-start | bytes 484
  48.2 3.7 %copy-start.8 = (f32[12]{0:T(128)}, f32[12]{0:T(128)S(1)}, u32[]{:S(2)}) copy-start(f32[12]{0:T(128)S(1)} %mul.413) | copy-start | bytes 148
  53.1 8.0 %collective-permute-start = (f32[19,16,1,128]{3,1,2,0:T(8,128)S(1)}, f32[19,16,1,128]{3,1,2,0:T(8,128)S(1)}, u32[]{:S(2)}, u32[]{:S(2)}) collective-permute-start(f32[19,16,1,128]{3,1,2,0:T(8,128)S(1)} %bitcast.405), channel_id=1, source_target_pairs={{0,4},{4,8},{8,12},{12,16},{16,20},{20,24},{24,28},{28,0},{1,5},{5... | collective-permute-start | bytes 466952 | tf_op jit(solution)/shard_map/ppermute | solution.py:43
  55.4 7.1 %collective-permute-start.1 = (f32[19,16,1,128]{3,1,2,0:T(8,128)S(1)}, f32[19,16,1,128]{3,1,2,0:T(8,128)S(1)}, u32[]{:S(2)}, u32[]{:S(2)}) collective-permute-start(f32[19,16,1,128]{3,1,2,0:T(8,128)S(1)} %bitcast.404), channel_id=1, source_target_pairs={{4,0},{8,4},{12,8},{16,12},{20,16},{24,20},{28,24},{0,28},{5,1},{9... | collective-permute-start | bytes 466952 | tf_op jit(solution)/shard_map/ppermute | solution.py:46
  61.2 1.4 %copy-start.3 = (f32[19,16,8,128]{3,2,1,0:T(8,128)}, f32[19,16,8,128]{3,2,1,0:T(8,128)S(1)}, u32[]{:S(2)}) copy-start(f32[19,16,8,128]{3,2,1,0:T(8,128)S(1)} %constant_dynamic-update-slice_fusion.36) | copy-start | bytes 3735556
  68.9 5.6 %collective-permute-start.2 = (f32[19,16,10,1]{0,1,3,2:T(8,128)S(1)}, f32[19,16,10,1]{0,1,3,2:T(8,128)S(1)}, u32[]{:S(2)}, u32[]{:S(2)}) collective-permute-start(f32[19,16,10,1]{0,1,3,2:T(8,128)S(1)} %copy.56), channel_id=1, source_target_pairs={{0,2},{2,0},{1,3},{3,1},{4,6},{6,4},{5,7},{7,5},{8,10},{10,8},{9,1... | collective-permute-start | bytes 36488 | tf_op jit(solution)/shard_map/ppermute | solution.py:43
  74.5 5.4 %collective-permute-start.3 = (f32[19,16,10,1]{0,1,3,2:T(8,128)S(1)}, f32[19,16,10,1]{0,1,3,2:T(8,128)S(1)}, u32[]{:S(2)}, u32[]{:S(2)}) collective-permute-start(f32[19,16,10,1]{0,1,3,2:T(8,128)S(1)} %copy.58), channel_id=1, source_target_pairs={{2,0},{0,2},{3,1},{1,3},{6,4},{4,6},{7,5},{5,7},{10,8},{8,10},{11,... | collective-permute-start | bytes 36488 | tf_op jit(solution)/shard_map/ppermute | solution.py:46
  83.6 2.4 %copy-start.1 = (f32[19,16,10,1]{3,2,1,0:T(8,128)S(1)}, f32[19,16,10,1]{3,2,1,0:T(8,128)}, u32[]{:S(2)}) copy-start(f32[19,16,10,1]{3,2,1,0:T(8,128)} %copy.59) | copy-start | bytes 36484
  85.4 2.8 %collective-permute-start.5 = (f32[19,1,10,130]{3,2,1,0:T(8,128)S(1)}, f32[19,1,10,130]{3,2,1,0:T(8,128)S(1)}, u32[]{:S(2)}, u32[]{:S(2)}) collective-permute-start(f32[19,1,10,130]{3,2,1,0:T(8,128)S(1)} %get-tuple-element.15), channel_id=1, source_target_pairs={{1,0},{0,1},{3,2},{2,3},{5,4},{4,5},{7,6},{6,7},{9,8},{8,9},{11,10... | collective-permute-start | bytes 296408 | tf_op jit(solution)/shard_map/ppermute | solution.py:46
  85.4 2.0 %copy-start = (f32[19,16,10,1]{3,2,1,0:T(8,128)S(1)}, f32[19,16,10,1]{3,2,1,0:T(8,128)}, u32[]{:S(2)}) copy-start(f32[19,16,10,1]{3,2,1,0:T(8,128)} %copy.57) | copy-start | bytes 36484
  85.5 2.0 %collective-permute-start.4 = (f32[19,1,10,130]{3,2,1,0:T(8,128)S(1)}, f32[19,1,10,130]{3,2,1,0:T(8,128)S(1)}, u32[]{:S(2)}, u32[]{:S(2)}) collective-permute-start(f32[19,1,10,130]{3,2,1,0:T(8,128)S(1)} %get-tuple-element.16), channel_id=1, source_target_pairs={{0,1},{1,0},{2,3},{3,2},{4,5},{5,4},{6,7},{7,6},{8,9},{9,8},{10,11... | collective-permute-start | bytes 296408 | tf_op jit(solution)/shard_map/ppermute | solution.py:43
where the time goes:
time: 98.2 us; the launch traced here: 97.8 us
  blocking collectives  42 us (43%)
  other arithmetic  22.3 us (23%)
  local copies, waits for them, and re-layouts  19.7 us (20%)
  starting transfers between devices  7.45 us (8%)
  waiting for transfers between devices  5.39 us (5%)
  between operations  0.99 us (1%)
    psum x1, blocking collectives, per_device(): panel_force = lax.psum(partial_force, ('gx', 'gy', 'gz'))  42 us
    unnamed x34, other arithmetic  13.4 us
    slice x3, local copies, waits for them, and re-layouts, padded_2(): lax.slice_in_dim(block, 0, width, axis=dim)  6.12 us
    ppermute x3, starting transfers between devices, padded_2(): lax.ppermute(lax.slice_in_dim(block, block.shape[dim] - width, None, axis...  4.86 us
    ppermute x3, waiting for transfers between devices, padded_2(): lax.ppermute(lax.slice_in_dim(block, block.shape[dim] - width, None, axis...  4.05 us
    ppermute x1, local copies, waits for them, and re-layouts, padded_2(): lax.ppermute(lax.slice_in_dim(block, block.shape[dim] - width, None, axis...  3.71 us
    ppermute x1, local copies, waits for them, and re-layouts, padded_2(): lax.ppermute(lax.slice_in_dim(block, 0, width, axis=dim), axis, backward)  3.7 us
    scatter-add x1, other arithmetic, per_device(): jnp.zeros_like(flat_density).at[cell_list].add(values)  3.28 us
  transfers between devices with their start and end apart: 6, of which 3 were waited for; matrix products, arithmetic and copies ran while one was open for 11% of the time, Pallas kernels for 0%

commit v1 on v0

v1 whole, which is shorter than its diff:
```python
import functools

import jax
import jax.numpy as jnp
from jax import lax
from jax.experimental import pallas as pl
from jax.experimental.pallas import tpu as pltpu
from jax.sharding import PartitionSpec as P

PANELS = 40
MODES = 12
VELOCITY = (
    (0, 0, 0),
    (1, 0, 0),
    (-1, 0, 0),
    (0, 1, 0),
    (0, -1, 0),
    (0, 0, 1),
    (0, 0, -1),
    (1, 1, 0),
    (-1, -1, 0),
    (1, -1, 0),
    (-1, 1, 0),
    (1, 0, 1),
    (-1, 0, -1),
    (1, 0, -1),
    (-1, 0, 1),
    (0, 1, 1),
    (0, -1, -1),
    (0, 1, -1),
    (0, -1, 1),
)
WEIGHTS = (1.0 / 3.0,) + (1.0 / 18.0,) * 6 + (1.0 / 36.0,) * 12
OMEGA = 1.0 / 0.6
WALL_SCALE = 0.02
COEF = tuple(6.0 * w * v[0] for w, v in zip(WEIGHTS, VELOCITY))
SIGNS = (1, -1)


def moving(axis, sign):
    return tuple(i for i in range(19) if VELOCITY[i][axis] == sign)


X_GROUP = tuple(moving(0, s) for s in SIGNS)
Y_GROUP = tuple(moving(1, s) for s in SIGNS)
Z_GROUP = tuple(moving(2, s) for s in SIGNS)
ORDER = Z_GROUP[0] + Z_GROUP[1] + tuple(i for i in range(19) if VELOCITY[i][2] == 0)
PLACE = tuple(ORDER.index(i) for i in range(19))
AXES = ("gx", "gy", "gz")
STAGES = (("gx",), ("gy", "gz"))
MESH = pl.DeviceIdType.MESH
F32 = jnp.float32
BF16 = jnp.bfloat16


def halves(x):
    high = x.astype(BF16)
    return high, (x - high.astype(F32)).astype(BF16)


def dot(a, b):
    return jnp.dot(a, b, preferred_element_type=F32)


def dot_nt(a, b):
    return lax.dot_general(a, b, (((1,), (1,)), ((), ())), preferred_element_type=F32)


def shift_of(velocity):
    return (velocity[0], velocity[1], velocity[2])


def offsets_of(sizes):
    found = []
    for i in range(1, 19):
        found.append(tuple(c % n for c, n in zip(VELOCITY[i], sizes)))
    for stage in STAGES:
        for offset in stage_offsets(stage, sizes):
            found.append(offset)
    return sorted(set(found))


def stage_offsets(stage, sizes):
    result = [(0, 0, 0)]
    for dim, axis in enumerate(AXES):
        if axis in stage:
            result = [
                tuple(k if d == dim else o[d] for d in range(3))
                for o in result
                for k in range(sizes[dim])
            ]
    return [o for o in result if o != (0, 0, 0)]


def kernel(
    sizes,
    pops,
    solid,
    cell,
    panel,
    area,
    shapes,
    panel_mode,
    compliance,
    out,
    force_out,
    amp_out,
    post,
    dens,
    wall,
    xs,
    xh,
    wxs,
    wxh,
    ys,
    yh,
    yxh,
    yzh,
    ws,
    wh,
    wyx,
    slots_a,
    slots_b,
    send_sem,
    recv_sem,
    send_a,
    recv_a,
    send_b,
    recv_b,
):
    depth, rows, width = pops.shape[1:]
    cells = depth * rows
    here = tuple(lax.axis_index(a) for a in AXES)

    def at(offset):
        return tuple(lax.rem(h + o % n, n) if o % n else h for h, o, n in zip(here, offset, sizes))

    partners = offsets_of(sizes)
    barrier = pltpu.get_barrier_semaphore()
    for offset in partners:
        pl.semaphore_signal(barrier, inc=1, device_id=at(offset), device_id_type=MESH)

    lane = lax.broadcasted_iota(jnp.int32, (rows, width), 1)
    sub = lax.broadcasted_iota(jnp.int32, (rows, width), 0)

    def collide(z, packed):
        f = [pops[i, z] for i in range(19)]
        density = f[0]
        for i in range(1, 19):
            density = density + f[i]
        inverse = 1.0 / density
        u = []
        for axis in range(3):
            plus, minus = moving(axis, 1), moving(axis, -1)
            total = f[plus[0]] - f[minus[0]]
            for i, j in zip(plus[1:], minus[1:]):
                total = total + (f[i] - f[j])
            u.append(total * inverse)
        base = 1.0 - 1.5 * (u[0] * u[0] + u[1] * u[1] + u[2] * u[2])
        fixed = solid[z] == 1
        dens[z] = density
        scaled = [OMEGA * w * density for w in WEIGHTS]
        new = [None] * 19
        new[0] = jnp.where(fixed, f[0], (1.0 - OMEGA) * f[0] + scaled[0] * base)
        for i in range(1, 19, 2):
            proj = None
            for axis in range(3):
                comp = VELOCITY[i][axis]
                if comp:
                    term = u[axis] if comp == 1 else -u[axis]
                    proj = term if proj is None else proj + term
            even = scaled[i] * (base + 4.5 * (proj * proj))
            odd = scaled[i] * (3.0 * proj)
            new[i] = jnp.where(fixed, f[i + 1], (1.0 - OMEGA) * f[i] + (even + odd))
            new[i + 1] = jnp.where(fixed, f[i], (1.0 - OMEGA) * f[i + 1] + (even - odd))
        for i in range(19):
            post[PLACE[i], z + 1] = new[i]
        packed = list(packed)
        for a in range(2):
            edge = rows - 1 if a == 0 else 0
            for k, i in enumerate(X_GROUP[a]):
                xs[a, k, z] = new[i][edge : edge + 1]
            edge = width - 1 if a == 0 else 0
            for j, i in enumerate(Y_GROUP[a]):
                column = jnp.broadcast_to(new[i][:, edge : edge + 1], (rows, width))
                packed[a] = jnp.where(lane == j * depth + z, column, packed[a])
        return tuple(packed)

    zero = jnp.zeros((rows, width), F32)
    packed = lax.fori_loop(0, depth, collide, (zero, zero))
    for a in range(2):
        ys[a] = packed[a]

    live = panel[...] >= 0
    col = lax.rem(cell[...], width)
    row = lax.div(cell[...], width)
    n_surf = cell.shape[1]
    pick_col = jnp.where(
        lax.broadcasted_iota(jnp.int32, (width, n_surf), 0) == col, 1.0, 0.0
    ).astype(BF16)
    on_row = lax.broadcasted_iota(jnp.int32, (cells, n_surf), 0) == row
    gauge_high, gauge_low = halves(dens[...].reshape(cells, width) - 1.0)
    by_row = dot(gauge_high, pick_col) + dot(gauge_low, pick_col)
    excess = jnp.sum(jnp.where(on_row, by_row, 0.0), axis=0, keepdims=True)
    contrib = jnp.where(live, area[...] * (excess / 3.0), 0.0)
    pick_panel = jnp.where(
        lax.broadcasted_iota(jnp.int32, (width, n_surf), 0) == panel[...], 1.0, 0.0
    ).astype(BF16)
    contrib_high, contrib_low = halves(jnp.broadcast_to(contrib, (8, n_surf)))
    partial = dot_nt(contrib_high, pick_panel) + dot_nt(contrib_low, pick_panel)
    partial = partial[0:1]

    pl.semaphore_wait(barrier, len(partners))

    def stage_start(stage, slots, send, recv, value):
        index = 0
        for dim, axis in enumerate(AXES):
            if axis in stage:
                index = index * sizes[dim] + here[dim]
        slots[index] = value
        copies = []
        for n, offset in enumerate(stage_offsets(stage, sizes)):
            copy = pltpu.make_async_remote_copy(
                src_ref=slots.at[index],
                dst_ref=slots.at[index],
                send_sem=send.at[n],
                recv_sem=recv.at[n],
                device_id=at(offset),
                device_id_type=MESH,
            )
            copy.start()
            copies.append(copy)
        return copies

    def stage_sum(slots, copies):
        for copy in copies:
            copy.wait()
        total = slots[0]
        for n in range(1, slots.shape[0]):
            total = total + slots[n]
        return total

    copies_a = stage_start(STAGES[0], slots_a, send_a, recv_a, partial)

    halo = []

    def send(src, dst, offset):
        copy = pltpu.make_async_remote_copy(
            src_ref=src,
            dst_ref=dst,
            send_sem=send_sem.at[len(halo)],
            recv_sem=recv_sem.at[len(halo)],
            device_id=at(offset),
            device_id_type=MESH,
        )
        copy.start()
        halo.append(copy)
        return copy

    for a, s in enumerate(SIGNS):
        group = Z_GROUP[a]
        first = a * len(group)
        source, target = (depth, 0) if a == 0 else (1, depth + 1)
        send(xs.at[a], xh.at[a, :, pl.ds(1, depth)], (s, 0, 0))
        send(
            post.at[pl.ds(first, len(group)), source],
            post.at[pl.ds(first, len(group)), target],
            (0, 0, s),
        )
        send(ys.at[a], yh.at[a], (0, s, 0))
        for b, t in enumerate(SIGNS):
            send(ys.at[a], yxh.at[a, b], (t, s, 0))
            send(ys.at[a], yzh.at[a, b], (0, s, t))
            k = [i for i in range(5) if VELOCITY[X_GROUP[a][i]][2] == t][0]
            source, target = (depth - 1, 0) if b == 0 else (0, depth + 1)
            send(xs.at[a, k, source], xh.at[a, k, target], (s, 0, t))

    mode_id = lax.broadcasted_iota(jnp.int32, (MODES, PANELS), 0)
    diagonal = lax.broadcasted_iota(jnp.int32, (MODES, MODES), 0) == lax.broadcasted_iota(
        jnp.int32, (MODES, MODES), 1
    )
    factor = jnp.sum(jnp.where(diagonal, compliance[...], 0.0), axis=1, keepdims=True)
    drives = panel_mode[...] == mode_id

    load_a = stage_sum(slots_a, copies_a)
    copies_b = stage_start(STAGES[1], slots_b, send_b, recv_b, load_a)
    force = stage_sum(slots_b, copies_b)[:, :PANELS]
    force_out[...] = force
    amp = factor * jnp.sum(jnp.where(drives, force, 0.0), axis=1, keepdims=True)
    amp_out[...] = jnp.sum(jnp.where(diagonal, amp, 0.0), axis=0, keepdims=True)

    speed = WALL_SCALE * jnp.sum(amp * shapes[...], axis=0, keepdims=True)
    speed = jnp.where(live, speed, 0.0)
    high, low = halves(jnp.where(on_row, speed, 0.0))
    flux = dot_nt(high, pick_col) + dot_nt(low, pick_col)
    flux = flux.reshape(depth, rows, width) * dens[...]
    wall[pl.ds(1, depth)] = flux

    def pack_wall(z, packed):
        value = wall[z + 1]
        packed = list(packed)
        for a in range(2):
            edge = rows - 1 if a == 0 else 0
            wxs[a, z] = value[edge : edge + 1]
            edge = width - 1 if a == 0 else 0
            column = jnp.broadcast_to(value[:, edge : edge + 1], (rows, width))
            for j, i in enumerate(Y_GROUP[a]):
                if VELOCITY[i][0]:
                    packed[a] = jnp.where(lane == j * depth + z, COEF[i] * column, packed[a])
        return tuple(packed)

    packed = lax.fori_loop(0, depth, pack_wall, (zero, zero))
    n_post = len(halo)
    for a, s in enumerate(SIGNS):
        ws[a] = packed[a]
        source, target = (depth, 0) if a == 0 else (1, depth + 1)
        send(wxs.at[a], wxh.at[a, pl.ds(1, depth)], (s, 0, 0))
        send(wall.at[source], wall.at[target], (0, 0, s))
        send(ws.at[a], wh.at[a], (0, s, 0))
        for b, t in enumerate(SIGNS):
            send(ws.at[a], wyx.at[a, b], (t, s, 0))
            source, target = (depth - 1, 0) if b == 0 else (0, depth + 1)
            send(wxs.at[a, source], wxh.at[a, target], (s, 0, t))

    for copy in halo:
        copy.wait()

    columns = []
    for a in range(2):
        face = yh[a] + wh[a]
        result = face
        for j, i in enumerate(Y_GROUP[a]):
            cx, _, cz = VELOCITY[i]
            mine = (lane >= j * depth) & (lane < (j + 1) * depth)
            if cx:
                b = SIGNS.index(cx)
                edge = yxh[a, b] + wyx[a, b]
                whole = pltpu.roll(face, cx % rows, 0)
                whole = jnp.where(sub == (0 if cx == 1 else rows - 1), pltpu.roll(edge, cx % rows, 0), whole)
                result = jnp.where(mine, whole, result)
            if cz:
                b = SIGNS.index(cz)
                whole = pltpu.roll(face, cz % width, 1)
                wrapped = pltpu.roll(yzh[a, b], (-cz * (depth - 1)) % width, 1)
                spot = j * depth if cz == 1 else (j + 1) * depth - 1
                result = jnp.where(mine, jnp.where(lane == spot, wrapped, whole), result)
        columns.append(result)

    def finish(z, columns):
        for i in range(19):
            cx, cy, cz = VELOCITY[i]
            source = z + 1 - cz
            value = post[PLACE[i], source]
            if cx:
                a = SIGNS.index(cx)
                k = X_GROUP[a].index(i)
                value = value + COEF[i] * wall[source]
                line = xh[a, k, source] + COEF[i] * wxh[a, source]
                value = pltpu.roll(value, cx % rows, 0)
                value = jnp.where(sub == (0 if cx == 1 else rows - 1), line, value)
            if cy:
                a = SIGNS.index(cy)
                j = Y_GROUP[a].index(i)
                value = pltpu.roll(value, cy % width, 1)
                column = jnp.broadcast_to(
                    columns[a][:, j * depth : j * depth + 1], (rows, width)
                )
                value = jnp.where(lane == (0 if cy == 1 else width - 1), column, value)
            out[i, z] = value
        return tuple(pltpu.roll(c, width - 1, 1) for c in columns)

    lax.fori_loop(0, depth, finish, tuple(columns))


def per_device(sizes, pops, solid, cell, panel, area, shapes, panel_mode, compliance):
    depth, rows, width = pops.shape[1:]
    n_surf = cell.shape[-1]
    count = {a: n for a, n in zip(AXES, sizes)}
    n_a, n_b = (
        functools.reduce(lambda x, y: x * y, [count[a] for a in stage]) for stage in STAGES
    )
    vmem = pl.BlockSpec(memory_space=pltpu.VMEM)
    tile = (rows, width)
    messages = 18 + 14
    dma = pltpu.SemaphoreType.DMA
    read, force, amp = pl.pallas_call(
        functools.partial(kernel, sizes),
        out_shape=(
            jax.ShapeDtypeStruct(pops.shape, F32),
            jax.ShapeDtypeStruct((1, PANELS), F32),
            jax.ShapeDtypeStruct((1, MODES), F32),
        ),
        in_specs=[vmem] * 8,
        out_specs=(vmem,) * 3,
        scratch_shapes=[
            pltpu.VMEM((19, depth + 2) + tile, F32),
            pltpu.VMEM((depth,) + tile, F32),
            pltpu.VMEM((depth + 2,) + tile, F32),
            pltpu.VMEM((2, 5, depth, 1, width), F32),
            pltpu.VMEM((2, 5, depth + 2, 1, width), F32),
            pltpu.VMEM((2, depth, 1, width), F32),
            pltpu.VMEM((2, depth + 2, 1, width), F32),
            pltpu.VMEM((2,) + tile, F32),
            pltpu.VMEM((2,) + tile, F32),
            pltpu.VMEM((2, 2) + tile, F32),
            pltpu.VMEM((2, 2) + tile, F32),
            pltpu.VMEM((2,) + tile, F32),
            pltpu.VMEM((2,) + tile, F32),
            pltpu.VMEM((2, 2) + tile, F32),
            pltpu.VMEM((n_a, 1, width), F32),
            pltpu.VMEM((n_b, 1, width), F32),
            dma((messages,)),
            dma((messages,)),
            dma((n_a - 1,)),
            dma((n_a - 1,)),
            dma((n_b - 1,)),
            dma((n_b - 1,)),
        ],
        compiler_params=pltpu.CompilerParams(
            collective_id=0, has_side_effects=True, vmem_limit_bytes=32 * 1024 * 1024
        ),
    )(
        pops,
        solid,
        cell.reshape(1, n_surf),
        panel.reshape(1, n_surf),
        area.reshape(1, n_surf),
        shapes.reshape(MODES, n_surf),
        panel_mode.reshape(1, PANELS),
        compliance.reshape(1, MODES),
    )
    return read, force.reshape(PANELS), amp.reshape(MODES)


def solution(mesh):
    placed = (
        P(None, "gz", "gx", "gy"),
        P("gz", "gx", "gy"),
        P("gz", "gx", "gy", None),
        P("gz", "gx", "gy", None),
        P("gz", "gx", "gy", None),
        P("gz", "gx", "gy", None, None),
        P(),
        P(),
    )
    return jax.shard_map(
        functools.partial(per_device, tuple(mesh.shape[a] for a in AXES)),
        mesh=mesh,
        in_specs=placed,
        out_specs=(P(None, "gz", "gx", "gy"), P(), P()),
        check_vma=False,
    )
```

time: 98.2 us -> 31.3 us (0.32)
  blocking collectives: 42 us -> 0 us
  other arithmetic: 22.3 us -> 0 us
  Pallas kernels: 0 us -> 22 us
  local copies, waits for them, and re-layouts: 19.7 us -> 8.29 us
  starting transfers between devices: 7.45 us -> 0 us
  waiting for transfers between devices: 5.39 us -> 0 us
    psum x1 -> x0, blocking collectives: 42 us -> none  [per_device(): panel_force = lax.psum(partial_force, ('gx', 'gy', 'gz'))]
    pallas_call x0 -> x1, Pallas kernels: none -> 22 us  [per_device(): pl.pallas_call(functools.partial(kernel, sizes), out_shape=(jax.ShapeDtyp...]
    unnamed x34 -> x0, other arithmetic: 13.4 us -> none
    slice x4 -> x0, local copies, waits for them, and re-layouts: 8.96 us -> none  [the longest x3 6.12 us: padded_2(): lax.slice_in_dim(block, 0, width, axis=dim)]
    unnamed x26 -> x18, local copies, waits for them, and re-layouts: 0.18 us -> 8.29 us
    ppermute x6 -> x0, starting transfers between devices: 7.45 us -> none  [the longest x3 4.86 us: padded_2(): lax.ppermute(lax.slice_in_dim(block, block.shape[dim] - width, None, axis...]
    ppermute x2 -> x0, local copies, waits for them, and re-layouts: 7.4 us -> none  [the longest x1 3.71 us: padded_2(): lax.ppermute(lax.slice_in_dim(block, block.shape[dim] - width, None, axis...]
    ppermute x6 -> x0, waiting for transfers between devices: 5.39 us -> none  [the longest x3 4.05 us: padded_2(): lax.ppermute(lax.slice_in_dim(block, block.shape[dim] - width, None, axis...]
  transfers between devices with their start and end apart: 6 -> 0, of which waited for: 3 -> 0; matrix products, arithmetic and copies ran while one was open for 11% -> 0% of each run, Pallas kernels for 0% -> 0%
where the time goes in v1:
time: 31.3 us; the launch traced here: 30.9 us
  Pallas kernels  22 us (70%)
  local copies, waits for them, and re-layouts  8.29 us (26%)
  between operations  0.65 us (2%)
    pallas_call x1, Pallas kernels, per_device(): pl.pallas_call(functools.partial(kernel, sizes), out_shape=(jax.ShapeDtyp...  22 us
    unnamed x18, local copies, waits for them, and re-layouts  8.29 us

profile of v1, /device:TPU:0, one launch (start us, length us, event | category | flops | bytes accessed | tf_op | source)
XLA Modules:
  0.0 30.9 jit_solution(17262221720845120062)
XLA Ops:
  0.6 0.7 %copy.13 = f32[1,1,1,12,512]{4,3,2,1,0:T(8,128)S(1)} copy(f32[1,1,1,12,512]{4,2,3,1,0:T(1,128)} %param.13) | data formatting | bytes 49152
  1.4 0.0 copy-start
  1.4 1.3 %copy-done = f32[19,16,8,128]{3,2,1,0:T(8,128)S(1)} copy-done((f32[19,16,8,128]{3,2,1,0:T(8,128)S(1)}, f32[19,16,8,128]{3,2,1,0:T(8,128)}, u32[]{:S(2)}) %copy-start) | copy-done | bytes 1245208
  2.7 0.0 copy-start.1
  2.7 0.8 %copy-done.1 = s32[16,8,128]{2,1,0:T(8,128)S(1)} copy-done((s32[16,8,128]{2,1,0:T(8,128)S(1)}, s32[16,8,128]{2,1,0:T(8,128)}, u32[]{:S(2)}) %copy-start.1) | copy-done | bytes 65560
  3.5 0.0 copy-start.2
  3.5 0.7 %copy-done.2 = s32[1,1,1,512]{3,2,1,0:T(1,128)S(1)} copy-done((s32[1,1,1,512]{3,2,1,0:T(1,128)S(1)}, s32[1,1,1,512]{3,2,1,0:T(1,128)}, u32[]{:S(2)}) %copy-start.2) | copy-done | bytes 2072
  4.2 0.0 copy-start.3
  4.2 0.7 %copy-done.3 = s32[1,1,1,512]{3,2,1,0:T(1,128)S(1)} copy-done((s32[1,1,1,512]{3,2,1,0:T(1,128)S(1)}, s32[1,1,1,512]{3,2,1,0:T(1,128)}, u32[]{:S(2)}) %copy-start.3) | copy-done | bytes 2072
  4.9 0.0 copy-start.4
  4.9 0.7 %copy-done.4 = f32[1,1,1,512]{3,2,1,0:T(1,128)S(1)} copy-done((f32[1,1,1,512]{3,2,1,0:T(1,128)S(1)}, f32[1,1,1,512]{3,2,1,0:T(1,128)}, u32[]{:S(2)}) %copy-start.4) | copy-done | bytes 2072
  5.6 0.0 copy-start.5
  5.6 0.7 %copy-done.5 = s32[40]{0:T(128)S(1)} copy-done((s32[40]{0:T(128)S(1)}, s32[40]{0:T(128)}, u32[]{:S(2)}) %copy-start.5) | copy-done | bytes 184
  6.2 0.0 copy-start.6
  6.2 0.7 %copy-done.6 = f32[12]{0:T(128)S(1)} copy-done((f32[12]{0:T(128)S(1)}, f32[12]{0:T(128)}, u32[]{:S(2)}) %copy-start.6) | copy-done | bytes 72
  6.9 22.0 %shard_map.103 = (f32[19,16,8,128]{3,2,1,0:T(8,128)S(1)}, f32[1,40]{1,0:T(1,128)S(1)}, f32[1,12]{1,0:T(1,128)S(1)}) custom-call(f32[19,16,8,128]{3,2,1,0:T(8,128)S(1)} %copy-done, s32[16,8,128]{2,1,0:T(8,128)S(1)} %copy-done.1, s32[1,512]{1,0:T(1,128)S(1)} %bitcast.11, s32[1,512]{1,0:T(1,128)S(1)} %bitcast.12, f32[1,512]{1,0:T(1,128)S(1)} %bitcast.13, ...), custom_call_target="tpu_custom_call" | custom-call | tf_op jit(solution)/shard_map/pallas_call | solution.py:386
  28.8 1.0 %copy.17 = f32[19,16,8,128]{3,2,1,0:T(8,128)} copy(f32[19,16,8,128]{3,2,1,0:T(8,128)S(1)} %get-tuple-element.12) | data formatting | bytes 2490368
  29.9 0.5 %copy.18 = f32[40]{0:T(128)} copy(f32[40]{0:T(128)S(1)} %bitcast.17) | data formatting | bytes 320
  30.4 0.5 %copy.19 = f32[12]{0:T(128)} copy(f32[12]{0:T(128)S(1)} %bitcast.16) | data formatting | bytes 96
Async XLA Ops:
  1.4 1.3 %copy-start = (f32[19,16,8,128]{3,2,1,0:T(8,128)S(1)}, f32[19,16,8,128]{3,2,1,0:T(8,128)}, u32[]{:S(2)}) copy-start(f32[19,16,8,128]{3,2,1,0:T(8,128)} %pops.1) | copy-start | bytes 3735556
  2.7 0.8 %copy-start.1 = (s32[16,8,128]{2,1,0:T(8,128)S(1)}, s32[16,8,128]{2,1,0:T(8,128)}, u32[]{:S(2)}) copy-start(s32[16,8,128]{2,1,0:T(8,128)} %solid.1) | copy-start | bytes 196612
  3.5 0.7 %copy-start.2 = (s32[1,1,1,512]{3,2,1,0:T(1,128)S(1)}, s32[1,1,1,512]{3,2,1,0:T(1,128)}, u32[]{:S(2)}) copy-start(s32[1,1,1,512]{3,2,1,0:T(1,128)} %param.10) | copy-start | bytes 6148
  4.2 0.7 %copy-start.3 = (s32[1,1,1,512]{3,2,1,0:T(1,128)S(1)}, s32[1,1,1,512]{3,2,1,0:T(1,128)}, u32[]{:S(2)}) copy-start(s32[1,1,1,512]{3,2,1,0:T(1,128)} %param.11) | copy-start | bytes 6148
  4.9 0.7 %copy-start.4 = (f32[1,1,1,512]{3,2,1,0:T(1,128)S(1)}, f32[1,1,1,512]{3,2,1,0:T(1,128)}, u32[]{:S(2)}) copy-start(f32[1,1,1,512]{3,2,1,0:T(1,128)} %param.12) | copy-start | bytes 6148
  5.6 0.7 %copy-start.5 = (s32[40]{0:T(128)S(1)}, s32[40]{0:T(128)}, u32[]{:S(2)}) copy-start(s32[40]{0:T(128)} %param.14) | copy-start | bytes 484
  6.2 0.7 %copy-start.6 = (f32[12]{0:T(128)S(1)}, f32[12]{0:T(128)}, u32[]{:S(2)}) copy-start(f32[12]{0:T(128)} %param.15) | copy-start | bytes 148

commit v2 on v1

v2 whole, which is shorter than its diff:
```python
import functools

import jax
import jax.numpy as jnp
from jax import lax
from jax.experimental import pallas as pl
from jax.experimental.pallas import tpu as pltpu
from jax.sharding import PartitionSpec as P

PANELS = 40
MODES = 12
VELOCITY = (
    (0, 0, 0),
    (1, 0, 0),
    (-1, 0, 0),
    (0, 1, 0),
    (0, -1, 0),
    (0, 0, 1),
    (0, 0, -1),
    (1, 1, 0),
    (-1, -1, 0),
    (1, -1, 0),
    (-1, 1, 0),
    (1, 0, 1),
    (-1, 0, -1),
    (1, 0, -1),
    (-1, 0, 1),
    (0, 1, 1),
    (0, -1, -1),
    (0, 1, -1),
    (0, -1, 1),
)
WEIGHTS = (1.0 / 3.0,) + (1.0 / 18.0,) * 6 + (1.0 / 36.0,) * 12
OMEGA = 1.0 / 0.6
WALL_SCALE = 0.02
COEF = tuple(6.0 * w * v[0] for w, v in zip(WEIGHTS, VELOCITY))
SIGNS = (1, -1)


def moving(axis, sign):
    return tuple(i for i in range(19) if VELOCITY[i][axis] == sign)


X_GROUP = tuple(moving(0, s) for s in SIGNS)
Y_GROUP = tuple(moving(1, s) for s in SIGNS)
Z_GROUP = tuple(moving(2, s) for s in SIGNS)
ORDER = Z_GROUP[0] + Z_GROUP[1] + tuple(i for i in range(19) if VELOCITY[i][2] == 0)
PLACE = tuple(ORDER.index(i) for i in range(19))
AXES = ("gx", "gy", "gz")
STAGES = (("gx",), ("gy", "gz"))
MESH = pl.DeviceIdType.MESH
N_LOADS = 4
F32 = jnp.float32
BF16 = jnp.bfloat16


def halves(x):
    high = x.astype(BF16)
    return high, (x - high.astype(F32)).astype(BF16)


def dot(a, b):
    return jnp.dot(a, b, preferred_element_type=F32)


def dot_nt(a, b):
    return lax.dot_general(a, b, (((1,), (1,)), ((), ())), preferred_element_type=F32)


def shift_of(velocity):
    return (velocity[0], velocity[1], velocity[2])


def offsets_of(sizes):
    found = []
    for i in range(1, 19):
        found.append(tuple(c % n for c, n in zip(VELOCITY[i], sizes)))
    for stage in STAGES:
        for offset in stage_offsets(stage, sizes):
            found.append(offset)
    return sorted(set(found))


def stage_offsets(stage, sizes):
    result = [(0, 0, 0)]
    for dim, axis in enumerate(AXES):
        if axis in stage:
            result = [
                tuple(k if d == dim else o[d] for d in range(3))
                for o in result
                for k in range(sizes[dim])
            ]
    return [o for o in result if o != (0, 0, 0)]


WALLS = []
for first, s in enumerate(SIGNS):
    WALLS.append(("x", first, 0, (s, 0, 0)))
    WALLS.append(("y", first, 0, (0, s, 0)))
    WALLS.append(("z", first, 0, (0, 0, s)))
    for second, t in enumerate(SIGNS):
        WALLS.append(("xz", first, second, (s, 0, t)))
        WALLS.append(("yx", first, second, (t, s, 0)))


def wall_offsets(sizes):
    return sorted({tuple(c % n for c, n in zip(w[3], sizes)) for w in WALLS})


def kernel(
    sizes,
    pops_in,
    solid_in,
    cell_in,
    panel_in,
    area_in,
    shapes_in,
    panel_mode_in,
    compliance_in,
    out,
    force_out,
    amp_out,
    pops,
    solid,
    cell,
    panel,
    area,
    shape_rows,
    panel_mode,
    compliance,
    mine,
    load_sem,
    post,
    dens,
    wall,
    xs,
    xh,
    wxh,
    ys,
    yh,
    yxh,
    yzh,
    theirs,
    picks,
    surf_send,
    surf_recv,
    slots_a,
    slots_b,
    send_sem,
    recv_sem,
    send_a,
    recv_a,
    send_b,
    recv_b,
):
    depth, rows, width = pops.shape[1:]
    cells = depth * rows
    here = tuple(lax.axis_index(a) for a in AXES)

    def at(offset):
        return tuple(lax.rem(h + o % n, n) if o % n else h for h, o, n in zip(here, offset, sizes))

    partners = offsets_of(sizes)
    barrier = pltpu.get_barrier_semaphore()
    for offset in partners:
        pl.semaphore_signal(barrier, inc=1, device_id=at(offset), device_id_type=MESH)

    pairs = [(cell_in, cell), (panel_in, panel), (area_in, area)]
    pairs += [(solid_in, solid), (shapes_in, shape_rows)]
    pairs += [(panel_mode_in, panel_mode), (compliance_in, compliance)]
    part = depth // N_LOADS
    cuts = [pl.ds(n * part, part) for n in range(N_LOADS)]
    pairs = pairs[:3] + [(pops_in.at[:, c], pops.at[:, c]) for c in cuts] + pairs[3:]
    loads = []
    for n, (src, dst) in enumerate(pairs):
        loads.append(pltpu.make_async_copy(src, dst, load_sem.at[n]))
        loads[n].start()

    lane = lax.broadcasted_iota(jnp.int32, (rows, width), 1)
    sub = lax.broadcasted_iota(jnp.int32, (rows, width), 0)

    for copy in loads[:3]:
        copy.wait()
    live = panel[...] >= 0
    col = lax.rem(cell[...], width)
    row = lax.div(cell[...], width)
    n_surf = cell.shape[1]
    pick_col = jnp.where(
        lax.broadcasted_iota(jnp.int32, (width, n_surf), 0) == col, 1.0, 0.0
    ).astype(BF16)
    on_row = lax.broadcasted_iota(jnp.int32, (cells, n_surf), 0) == row

    def add_up(z, carry):
        density = pops[0, z]
        for i in range(1, 19):
            density = density + pops[i, z]
        dens[z + 1] = density
        return carry

    for n in range(N_LOADS):
        loads[3 + n].wait()
        lax.fori_loop(n * part, (n + 1) * part, add_up, 0)
    gauge_high, gauge_low = halves(dens[pl.ds(1, depth)].reshape(cells, width) - 1.0)
    by_row = dot(gauge_high, pick_col) + dot(gauge_low, pick_col)
    excess = jnp.sum(jnp.where(on_row, by_row, 0.0), axis=0, keepdims=True)
    contrib = jnp.where(live, area[...] * (excess / 3.0), 0.0)
    pick_panel = jnp.where(
        lax.broadcasted_iota(jnp.int32, (width, n_surf), 0) == panel[...], 1.0, 0.0
    ).astype(BF16)
    contrib_high, contrib_low = halves(jnp.broadcast_to(contrib, (8, n_surf)))
    partial = dot_nt(contrib_high, pick_panel) + dot_nt(contrib_low, pick_panel)
    partial = partial[0:1]

    pl.semaphore_wait(barrier, len(partners))

    def stage_start(stage, slots, send, recv, value):
        index = 0
        for dim, axis in enumerate(AXES):
            if axis in stage:
                index = index * sizes[dim] + here[dim]
        slots[index] = value
        copies = []
        for n, offset in enumerate(stage_offsets(stage, sizes)):
            copy = pltpu.make_async_remote_copy(
                src_ref=slots.at[index],
                dst_ref=slots.at[index],
                send_sem=send.at[n],
                recv_sem=recv.at[n],
                device_id=at(offset),
                device_id_type=MESH,
            )
            copy.start()
            copies.append(copy)
        return copies

    def stage_sum(slots, copies):
        for copy in copies:
            copy.wait()
        total = slots[0]
        for n in range(1, slots.shape[0]):
            total = total + slots[n]
        return total

    copies_a = stage_start(STAGES[0], slots_a, send_a, recv_a, partial)

    for copy in loads[3 + N_LOADS :]:
        copy.wait()
    for m in range(MODES):
        mine[m : m + 1, :] = jnp.where(live, shape_rows[m], 0.0)
    mine[MODES : MODES + 1, :] = cell[...].astype(F32)
    mine[MODES + 1 :, :] = jnp.zeros((mine.shape[0] - MODES - 1, n_surf), F32)
    surfels = []
    for n, offset in enumerate(wall_offsets(sizes)):
        copy = pltpu.make_async_remote_copy(
            src_ref=mine,
            dst_ref=theirs.at[n],
            send_sem=surf_send.at[n],
            recv_sem=surf_recv.at[n],
            device_id=at(offset),
            device_id_type=MESH,
        )
        copy.start()
        surfels.append(copy)

    def collide(z, packed):
        f = [pops[i, z] for i in range(19)]
        density = dens[z + 1]
        inverse = 1.0 / density
        u = []
        for axis in range(3):
            plus, minus = moving(axis, 1), moving(axis, -1)
            total = f[plus[0]] - f[minus[0]]
            for i, j in zip(plus[1:], minus[1:]):
                total = total + (f[i] - f[j])
            u.append(total * inverse)
        base = 1.0 - 1.5 * (u[0] * u[0] + u[1] * u[1] + u[2] * u[2])
        fixed = solid[z] == 1
        scaled = [OMEGA * w * density for w in WEIGHTS]
        new = [None] * 19
        new[0] = jnp.where(fixed, f[0], (1.0 - OMEGA) * f[0] + scaled[0] * base)
        for i in range(1, 19, 2):
            proj = None
            for axis in range(3):
                comp = VELOCITY[i][axis]
                if comp:
                    term = u[axis] if comp == 1 else -u[axis]
                    proj = term if proj is None else proj + term
            even = scaled[i] * (base + 4.5 * (proj * proj))
            odd = scaled[i] * (3.0 * proj)
            new[i] = jnp.where(fixed, f[i + 1], (1.0 - OMEGA) * f[i] + (even + odd))
            new[i + 1] = jnp.where(fixed, f[i], (1.0 - OMEGA) * f[i + 1] + (even - odd))
        for i in range(19):
            post[PLACE[i], z + 1] = new[i]
        packed = list(packed)
        for a in range(2):
            edge = rows - 1 if a == 0 else 0
            for k, i in enumerate(X_GROUP[a]):
                xs[a, k, z] = new[i][edge : edge + 1]
            xs[a, 5, z] = density[edge : edge + 1]
            edge = width - 1 if a == 0 else 0
            for j, value in enumerate([new[i] for i in Y_GROUP[a]] + [density]):
                column = jnp.broadcast_to(value[:, edge : edge + 1], (rows, width))
                packed[a] = jnp.where(lane == j * depth + z, column, packed[a])
        return tuple(packed)

    zero = jnp.zeros((rows, width), F32)
    packed = lax.fori_loop(0, depth, collide, (zero, zero))
    for a in range(2):
        ys[a] = packed[a]

    halo = []

    def send(src, dst, offset):
        copy = pltpu.make_async_remote_copy(
            src_ref=src,
            dst_ref=dst,
            send_sem=send_sem.at[len(halo)],
            recv_sem=recv_sem.at[len(halo)],
            device_id=at(offset),
            device_id_type=MESH,
        )
        copy.start()
        halo.append(copy)
        return copy

    for a, s in enumerate(SIGNS):
        group = Z_GROUP[a]
        first = a * len(group)
        source, target = (depth, 0) if a == 0 else (1, depth + 1)
        send(xs.at[a], xh.at[a, :, pl.ds(1, depth)], (s, 0, 0))
        send(
            post.at[pl.ds(first, len(group)), source],
            post.at[pl.ds(first, len(group)), target],
            (0, 0, s),
        )
        send(dens.at[source], dens.at[target], (0, 0, s))
        send(ys.at[a], yh.at[a], (0, s, 0))
        for b, t in enumerate(SIGNS):
            send(ys.at[a], yxh.at[a, b], (t, s, 0))
            send(ys.at[a], yzh.at[a, b], (0, s, t))
            k = [i for i in range(5) if VELOCITY[X_GROUP[a][i]][2] == t][0]
            source, target = (depth - 1, 0) if b == 0 else (0, depth + 1)
            send(xs.at[a, k, source], xh.at[a, k, target], (s, 0, t))
            send(xs.at[a, 5, source], xh.at[a, 5, target], (s, 0, t))

    mode_id = lax.broadcasted_iota(jnp.int32, (MODES, PANELS), 0)
    diagonal = lax.broadcasted_iota(jnp.int32, (MODES, MODES), 0) == lax.broadcasted_iota(
        jnp.int32, (MODES, MODES), 1
    )
    factor = jnp.sum(jnp.where(diagonal, compliance[...], 0.0), axis=1, keepdims=True)
    drives = panel_mode[...] == mode_id

    load_a = stage_sum(slots_a, copies_a)
    copies_b = stage_start(STAGES[1], slots_b, send_b, recv_b, load_a)
    def arrived(moved):
        columns = []
        for a in range(2):
            face = yh[a] + y_flux[a] if moved else yh[a]
            result = face
            for j, i in enumerate(Y_GROUP[a]):
                cx, _, cz = VELOCITY[i]
                mine = (lane >= j * depth) & (lane < (j + 1) * depth)
                if cx and moved:
                    b = SIGNS.index(cx)
                    edge = pltpu.roll(yxh[a, b] + yx_flux[a][b], cx % rows, 0)
                    whole = pltpu.roll(face, cx % rows, 0)
                    whole = jnp.where(sub == (0 if cx == 1 else rows - 1), edge, whole)
                    result = jnp.where(mine, whole, result)
                if cz and not moved:
                    b = SIGNS.index(cz)
                    whole = pltpu.roll(face, cz % width, 1)
                    wrapped = pltpu.roll(yzh[a, b], (-cz * (depth - 1)) % width, 1)
                    spot = j * depth if cz == 1 else (j + 1) * depth - 1
                    whole = jnp.where(lane == spot, wrapped, whole)
                    result = jnp.where(mine, whole, result)
            columns.append(result)
        return columns

    def finish(moved, z, columns):
        for i in range(19):
            cx, cy, cz = VELOCITY[i]
            if bool(cx) != moved:
                continue
            source = z + 1 - cz
            value = post[PLACE[i], source]
            if cx:
                a = SIGNS.index(cx)
                k = X_GROUP[a].index(i)
                value = value + COEF[i] * wall[source]
                line = xh[a, k, source] + COEF[i] * wxh[a, source]
                value = pltpu.roll(value, cx % rows, 0)
                value = jnp.where(sub == (0 if cx == 1 else rows - 1), line, value)
            if cy:
                a = SIGNS.index(cy)
                j = Y_GROUP[a].index(i)
                value = pltpu.roll(value, cy % width, 1)
                column = jnp.broadcast_to(
                    columns[a][:, j * depth : j * depth + 1], (rows, width)
                )
                value = jnp.where(lane == (0 if cy == 1 else width - 1), column, value)
            out[i, z] = value
        return tuple(pltpu.roll(c, width - 1, 1) for c in columns)

    for copy in halo:
        copy.wait()
    lax.fori_loop(0, depth, functools.partial(finish, False), tuple(arrived(False)))

    for copy in surfels:
        copy.wait()
    masks = []
    places = wall_offsets(sizes)
    spot = lax.broadcasted_iota(jnp.int32, (width, n_surf), 0)
    spot_z = lax.rem(spot, depth)
    row_id = lax.broadcasted_iota(jnp.int32, (rows, n_surf), 0)
    level_id = lax.broadcasted_iota(jnp.int32, (depth, n_surf), 0)
    for index, (kind, a, b, velocity) in enumerate(WALLS):
        offset = places.index(tuple(c % n for c, n in zip(velocity, sizes)))
        cells_of = theirs[offset, MODES : MODES + 1, :].astype(jnp.int32)
        cy = lax.rem(cells_of, width)
        cx = lax.rem(lax.div(cells_of, width), rows)
        cz = lax.div(cells_of, width * rows)
        picked = (spot_z == cz) if kind[0] == "y" else (spot == cy)
        picks[index] = jnp.where(picked, 1.0, 0.0).astype(BF16)
        if kind == "x":
            mask = (level_id == cz) & (cx == (rows - 1 if a == 0 else 0))
        elif kind[0] == "y":
            mask = (row_id == cx) & (cy == (width - 1 if a == 0 else 0))
        else:
            up = a if kind == "z" else b
            mask = (row_id == cx) & (cz == (depth - 1 if up == 0 else 0))
        masks.append((mask, offset))

    force = stage_sum(slots_b, copies_b)[:, :PANELS]
    force_out[...] = force
    amp = factor * jnp.sum(jnp.where(drives, force, 0.0), axis=1, keepdims=True)
    amp_out[...] = jnp.sum(jnp.where(diagonal, amp, 0.0), axis=0, keepdims=True)

    def speed_of(block):
        return WALL_SCALE * jnp.sum(amp * block[:MODES, :], axis=0, keepdims=True)

    high, low = halves(jnp.where(on_row, speed_of(mine[...]), 0.0))
    flux = dot_nt(high, pick_col) + dot_nt(low, pick_col)
    flux = flux.reshape(depth, rows, width) * dens[pl.ds(1, depth)]
    wall[pl.ds(1, depth)] = flux

    speeds = [speed_of(theirs[n]) for n in range(len(surfels))]

    def spread(index, mask, offset):
        high, low = halves(jnp.where(mask, speeds[offset], 0.0))
        return dot_nt(high, picks[index]) + dot_nt(low, picks[index])

    def on_lanes(a, tile, flux):
        result = jnp.zeros_like(tile)
        for j, i in enumerate(Y_GROUP[a]):
            if VELOCITY[i][0]:
                mine_lanes = (lane >= j * depth) & (lane < (j + 1) * depth)
                moved = pltpu.roll(tile, (j - 5) * depth % width, 1)
                result = jnp.where(mine_lanes, COEF[i] * moved * flux, result)
        return result

    y_flux = [None, None]
    yx_flux = [[None, None], [None, None]]
    for index, (kind, a, b, velocity) in enumerate(WALLS):
        mask, offset = masks[index]
        flux = spread(index, mask, offset)
        if kind == "x":
            for z in range(depth):
                wxh[a, z + 1] = flux[z : z + 1] * xh[a, 5, z + 1]
        elif kind == "z":
            slot = 0 if a == 0 else depth + 1
            wall[slot] = flux * dens[slot]
        elif kind == "xz":
            edge = rows - 1 if a == 0 else 0
            slot = 0 if b == 0 else depth + 1
            wxh[a, slot] = flux[edge : edge + 1] * xh[a, 5, slot]
        elif kind == "y":
            y_flux[a] = on_lanes(a, yh[a], flux)
        else:
            yx_flux[a][b] = on_lanes(a, yxh[a, b], flux)

    columns = arrived(True)
    lax.fori_loop(0, depth, functools.partial(finish, True), tuple(columns))


def per_device(sizes, pops, solid, cell, panel, area, shapes, panel_mode, compliance):
    depth, rows, width = pops.shape[1:]
    n_surf = cell.shape[-1]
    count = {a: n for a, n in zip(AXES, sizes)}
    n_a, n_b = (
        functools.reduce(lambda x, y: x * y, [count[a] for a in stage]) for stage in STAGES
    )
    vmem = pl.BlockSpec(memory_space=pltpu.VMEM)
    tile = (rows, width)
    messages = 18 + 6
    n_wall = len(wall_offsets(sizes))
    dma = pltpu.SemaphoreType.DMA
    read, force, amp = pl.pallas_call(
        functools.partial(kernel, sizes),
        out_shape=(
            jax.ShapeDtypeStruct(pops.shape, F32),
            jax.ShapeDtypeStruct((1, PANELS), F32),
            jax.ShapeDtypeStruct((1, MODES), F32),
        ),
        in_specs=[pl.BlockSpec(memory_space=pltpu.HBM)] * 8,
        out_specs=(vmem,) * 3,
        scratch_shapes=[
            pltpu.VMEM(pops.shape, F32),
            pltpu.VMEM(solid.shape, jnp.int32),
            pltpu.VMEM((1, n_surf), jnp.int32),
            pltpu.VMEM((1, n_surf), jnp.int32),
            pltpu.VMEM((1, n_surf), F32),
            pltpu.VMEM((MODES, 1, n_surf), F32),
            pltpu.VMEM((1, PANELS), jnp.int32),
            pltpu.VMEM((1, MODES), F32),
            pltpu.VMEM((16, n_surf), F32),
            dma((7 + N_LOADS,)),
            pltpu.VMEM((19, depth + 2) + tile, F32),
            pltpu.VMEM((depth + 2,) + tile, F32),
            pltpu.VMEM((depth + 2,) + tile, F32),
            pltpu.VMEM((2, 6, depth, 1, width), F32),
            pltpu.VMEM((2, 6, depth + 2, 1, width), F32),
            pltpu.VMEM((2, depth + 2, 1, width), F32),
            pltpu.VMEM((2,) + tile, F32),
            pltpu.VMEM((2,) + tile, F32),
            pltpu.VMEM((2, 2) + tile, F32),
            pltpu.VMEM((2, 2) + tile, F32),
            pltpu.VMEM((n_wall, 16, n_surf), F32),
            pltpu.VMEM((len(WALLS), width, n_surf), BF16),
            dma((n_wall,)),
            dma((n_wall,)),
            pltpu.VMEM((n_a, 1, width), F32),
            pltpu.VMEM((n_b, 1, width), F32),
            dma((messages,)),
            dma((messages,)),
            dma((n_a - 1,)),
            dma((n_a - 1,)),
            dma((n_b - 1,)),
            dma((n_b - 1,)),
        ],
        compiler_params=pltpu.CompilerParams(
            collective_id=0, has_side_effects=True, vmem_limit_bytes=62 * 1024 * 1024
        ),
    )(
        pops,
        solid,
        cell.reshape(1, n_surf),
        panel.reshape(1, n_surf),
        area.reshape(1, n_surf),
        shapes.reshape(MODES, 1, n_surf),
        panel_mode.reshape(1, PANELS),
        compliance.reshape(1, MODES),
    )
    return read, force.reshape(PANELS), amp.reshape(MODES)


def solution(mesh):
    placed = (
        P(None, "gz", "gx", "gy"),
        P("gz", "gx", "gy"),
        P("gz", "gx", "gy", None),
        P("gz", "gx", "gy", None),
        P("gz", "gx", "gy", None),
        P("gz", "gx", "gy", None, None),
        P(),
        P(),
    )
    return jax.shard_map(
        functools.partial(per_device, tuple(mesh.shape[a] for a in AXES)),
        mesh=mesh,
        in_specs=placed,
        out_specs=(P(None, "gz", "gx", "gy"), P(), P()),
        check_vma=False,
    )
```

time: 31.3 us -> 25 us (0.80)
  local copies, waits for them, and re-layouts: 8.29 us -> 3.47 us
  Pallas kernels: 22 us -> 20.7 us
    unnamed x18 -> x7, local copies, waits for them, and re-layouts: 8.29 us -> 3.47 us
    pallas_call x1, Pallas kernels: 22 us -> 20.7 us  [per_device(): pl.pallas_call(functools.partial(kernel, sizes), out_shape=(jax.ShapeDtyp...]
where the time goes in v2:
time: 25 us; the launch traced here: 24.8 us
  Pallas kernels  20.7 us (83%)
  local copies, waits for them, and re-layouts  3.47 us (14%)
  between operations  0.66 us (3%)
    pallas_call x1, Pallas kernels, per_device(): pl.pallas_call(functools.partial(kernel, sizes), out_shape=(jax.ShapeDtyp...  20.7 us
    unnamed x7, local copies, waits for them, and re-layouts  3.47 us

profile of v2, /device:TPU:0, one launch (start us, length us, event | category | flops | bytes accessed | tf_op | source)
XLA Modules:
  0.0 24.8 jit_solution(9589902747411192255)
XLA Ops:
  0.6 20.7 %shard_map.103 = (f32[19,16,8,128]{3,2,1,0:T(8,128)}, f32[1,40]{1,0:T(1,128)}, f32[1,12]{1,0:T(1,128)}) custom-call(f32[19,16,8,128]{3,2,1,0:T(8,128)} %pops_in.1, s32[16,8,128]{2,1,0:T(8,128)} %solid_in.1, s32[1,512]{1,0:T(1,128)} %bitcast.9, s32[1,512]{1,0:T(1,128)} %bitcast.10, f32[1,512]{1,0:T(1,128)} %bitcast.11, f32[12,1,512]{2,1,0:T(1,128)} %bitcast.8, ...), custom_call_target="tpu_custom_call" | custom-call | tf_op jit(solution)/shard_map/pallas_call | solution.py:497
  21.3 0.0 copy-start.1
  21.3 0.0 copy-start
  21.3 2.4 %copy.14 = f32[19,16,8,128]{3,2,1,0:T(8,128)} copy(f32[19,16,8,128]{3,2,1,0:T(8,128)} %get-tuple-element.12) | data formatting | bytes 2490368
  23.8 0.0 copy-done.1
  23.8 0.5 %copy.15 = f32[40]{0:T(128)} copy(f32[40]{0:T(128)S(1)} %bitcast.15) | data formatting | bytes 320
  24.3 0.0 copy-done
  24.3 0.5 %copy.16 = f32[12]{0:T(128)} copy(f32[12]{0:T(128)S(1)} %bitcast.14) | data formatting | bytes 96
Async XLA Ops:
  21.3 2.5 %copy-start.1 = (f32[1,40]{1,0:T(1,128)S(1)}, f32[1,40]{1,0:T(1,128)}, u32[]{:S(2)}) copy-start(f32[1,40]{1,0:T(1,128)} %get-tuple-element.7) | copy-start | bytes 484
  21.3 3.0 %copy-start = (f32[1,12]{1,0:T(1,128)S(1)}, f32[1,12]{1,0:T(1,128)}, u32[]{:S(2)}) copy-start(f32[1,12]{1,0:T(1,128)} %get-tuple-element.8) | copy-start | bytes 148

commit v3 on v2

--- a/solution.py
+++ b/solution.py
@@ -199,7 +199,7 @@
 
     for n in range(N_LOADS):
         loads[3 + n].wait()
-        lax.fori_loop(n * part, (n + 1) * part, add_up, 0)
+        lax.fori_loop(n * part, (n + 1) * part, add_up, 0, unroll=True)
     gauge_high, gauge_low = halves(dens[pl.ds(1, depth)].reshape(cells, width) - 1.0)
     by_row = dot(gauge_high, pick_col) + dot(gauge_low, pick_col)
     excess = jnp.sum(jnp.where(on_row, by_row, 0.0), axis=0, keepdims=True)
@@ -479,7 +479,7 @@
             yx_flux[a][b] = on_lanes(a, yxh[a, b], flux)
 
     columns = arrived(True)
-    lax.fori_loop(0, depth, functools.partial(finish, True), tuple(columns))
+    lax.fori_loop(0, depth, functools.partial(finish, True), tuple(columns), unroll=2)
 
 
 def per_device(sizes, pops, solid, cell, panel, area, shapes, panel_mode, compliance):
@@ -538,17 +538,22 @@
             dma((n_b - 1,)),
         ],
         compiler_params=pltpu.CompilerParams(
-            collective_id=0, has_side_effects=True, vmem_limit_bytes=62 * 1024 * 1024
+            collective_id=0, has_side_effects=True, vmem_limit_bytes=32 * 1024 * 1024
         ),
     )(
-        pops,
-        solid,
-        cell.reshape(1, n_surf),
-        panel.reshape(1, n_surf),
-        area.reshape(1, n_surf),
-        shapes.reshape(MODES, 1, n_surf),
-        panel_mode.reshape(1, PANELS),
-        compliance.reshape(1, MODES),
+        *(
+            pltpu.with_memory_space_constraint(x, pltpu.HBM)
+            for x in (
+                pops,
+                solid,
+                cell.reshape(1, n_surf),
+                panel.reshape(1, n_surf),
+                area.reshape(1, n_surf),
+                shapes.reshape(MODES, 1, n_surf),
+                panel_mode.reshape(1, PANELS),
+                compliance.reshape(1, MODES),
+            )
+        )
     )
     return read, force.reshape(PANELS), amp.reshape(MODES)
 

time: 25 us -> 22.3 us (0.89)
  local copies, waits for them, and re-layouts: 3.47 us -> 2.06 us
  Pallas kernels: 20.7 us -> 19.4 us
    unnamed x7 -> x3, local copies, waits for them, and re-layouts: 3.47 us -> 2.06 us
    pallas_call x1, Pallas kernels: 20.7 us -> 19.4 us  [per_device(): pl.pallas_call(functools.partial(kernel, sizes), out_shape=(jax.ShapeDtyp...]
where the time goes in v3:
time: 22.3 us; the launch traced here: 22.1 us
  Pallas kernels  19.4 us (87%)
  local copies, waits for them, and re-layouts  2.06 us (9%)
  between operations  0.64 us (3%)
    pallas_call x1, Pallas kernels, per_device(): pl.pallas_call(functools.partial(kernel, sizes), out_shape=(jax.ShapeDtyp...  19.4 us
    unnamed x3, local copies, waits for them, and re-layouts  2.06 us

profile of v3, /device:TPU:0, one launch (start us, length us, event | category | flops | bytes accessed | tf_op | source)
XLA Modules:
  0.0 22.1 jit_solution(666234826725314372)
XLA Ops:
  0.6 19.4 %shard_map.103 = (f32[19,16,8,128]{3,2,1,0:T(8,128)S(1)}, f32[1,40]{1,0:T(1,128)S(1)}, f32[1,12]{1,0:T(1,128)S(1)}) custom-call(f32[19,16,8,128]{3,2,1,0:T(8,128)} %pops_in.1, s32[16,8,128]{2,1,0:T(8,128)} %solid_in.1, s32[1,512]{1,0:T(1,128)} %bitcast.11, s32[1,512]{1,0:T(1,128)} %bitcast.12, f32[1,512]{1,0:T(1,128)} %bitcast.13, f32[12,1,512]{2,1,0:T(1,128)} %bitcast.10, ...), custom_call_target="tpu_custom_call" | custom-call | tf_op jit(solution)/shard_map/pallas_call | solution.py:497
  20.0 1.0 %copy.14 = f32[19,16,8,128]{3,2,1,0:T(8,128)} copy(f32[19,16,8,128]{3,2,1,0:T(8,128)S(1)} %get-tuple-element.12) | data formatting | bytes 2490368
  21.1 0.5 %copy.15 = f32[40]{0:T(128)} copy(f32[40]{0:T(128)S(1)} %bitcast.9) | data formatting | bytes 320
  21.6 0.5 %copy.16 = f32[12]{0:T(128)} copy(f32[12]{0:T(128)S(1)} %bitcast.8) | data formatting | bytes 96
